TPU v7x, 32 devices: a whole 2x2x4 slice. The times are simulated.
32 devices in a mesh: batch: 8 (over y, x, core), blk: 4 (over z).
Axes of the slice: x: 2, y: 2, z: 4, core: 2. Of those that a mesh axis runs over, the one named last changes fastest.
Arguments:
- tokens: bfloat16 [32, 640, 768], P('batch', 'blk'), may hold values from -6 to 6
- resolution: int32 [32], P('batch'), may hold values from 0 to 1, as said below
- positions: int32 [32, 640], P('batch'), may hold values from 0 to 575, as said below
- ln1_gain: bfloat16 [768], replicated, may hold values from 0.5 to 1.5
- ln1_bias: bfloat16 [768], replicated, may hold values from -1.75 to 1.75
- w_qkv: bfloat16 [768, 2304], replicated, may hold values from -0.21875 to 0.21875
- q_bias: bfloat16 [768], replicated, may hold values from -3 to 3
- v_bias: bfloat16 [768], replicated, may hold values from -0.625 to 0.625
- w_proj: bfloat16 [768, 768], replicated, may hold values from -1.75 to 1.75
- proj_bias: bfloat16 [768], replicated, may hold values from -1.75 to 1.75
- gamma1: bfloat16 [768], replicated, may hold values from 0.5 to 2
- ln2_gain: bfloat16 [768], replicated, may hold values from 0.5 to 1.5
- ln2_bias: bfloat16 [768], replicated, may hold values from -1.75 to 1.75
- w_fc1: bfloat16 [768, 3072], replicated, may hold values from -0.21875 to 0.21875
- fc1_bias: bfloat16 [3072], replicated, may hold values from -3 to 3
- w_fc2: bfloat16 [3072, 768], replicated, may hold values from -0.109375 to 0.109375
- fc2_bias: bfloat16 [768], replicated, may hold values from -1.75 to 1.75
- gamma2: bfloat16 [768], replicated, may hold values from 0.5 to 2
- rel_low: bfloat16 [732, 12], replicated, may hold values from -4 to 4
- rel_high: bfloat16 [2212, 12], replicated, may hold values from -4 to 4
- grad_out: bfloat16 [32, 640, 768], P('batch', 'blk'), may hold values from -6 to 6
Outputs:
- output: bfloat16 [32, 640, 768], P('batch', 'blk')
- grad_tokens: bfloat16 [32, 640, 768], P('batch', 'blk')
- grad_ln1_gain: float32 [768], replicated
- grad_ln1_bias: float32 [768], replicated
- grad_w_qkv: float32 [768, 2304], P(('batch', 'blk'))
- grad_q_bias: float32 [768], replicated
- grad_v_bias: float32 [768], replicated
- grad_w_proj: float32 [768, 768], P(('batch', 'blk'))
- grad_proj_bias: float32 [768], replicated
- grad_gamma1: float32 [768], replicated
- grad_ln2_gain: float32 [768], replicated
- grad_ln2_bias: float32 [768], replicated
- grad_w_fc1: float32 [768, 3072], P(('batch', 'blk'))
- grad_fc1_bias: float32 [3072], replicated
- grad_w_fc2: float32 [3072, 768], P(('batch', 'blk'))
- grad_fc2_bias: float32 [768], replicated
- grad_gamma2: float32 [768], replicated
- grad_rel_low: float32 [732, 12], replicated
- grad_rel_high: float32 [2212, 12], replicated
Inputs may be any that keep to these rules, and one draw needn't show every extreme that they name: Among each 4 consecutive images (those of one index of batch) at least one has resolution 1. `positions`: for an image of grid side G, entries 1 to G * G hold every cell 0 to G * G - 1 once (cell = row * G + column); all other entries are 0.
All inputs are finite; a program needn't handle non-finite values.
Results may differ from a plain program's by a relative error of at most 0.015.
Values may be sent and summed in bfloat16 or wider, within the bound.
A program may use at most 384 MiB of HBM per device.

v0:
```python
import jax
import jax.numpy as jnp
from jax import lax
from jax.sharding import PartitionSpec as P

G_LOW = 14
G_HIGH = 24


def layer_stats(values):
    center = values - jnp.mean(values, axis=-1, keepdims=True)
    factor = lax.rsqrt(jnp.mean(center * center, axis=-1, keepdims=True) + 1e-06)
    return (center * factor, factor)


def norm_back(grad, normed, factor, gain):
    scaled = grad * gain
    return factor * (
        scaled
        - jnp.mean(scaled, axis=-1, keepdims=True)
        - normed * jnp.mean(scaled * normed, axis=-1, keepdims=True)
    )


def gelu_slope(values):
    return (
        0.5 * (1.0 + lax.erf(values * 0.7071067811865476))
        + values * jnp.exp(-0.5 * values * values) * 0.3989422804014327
    )


def matmul(left, right):
    return jnp.dot(left, right, preferred_element_type=jnp.float32)


def weight_grad(left, right):
    return jnp.einsum("nd,ne->de", left, right, preferred_element_type=jnp.float32)


def offset_table(grid):
    side = 2 * grid - 1
    offsets = jnp.arange(side, dtype=jnp.int32)
    places = jnp.arange(grid, dtype=jnp.int32)
    return (
        places[None, :, None] - places[None, None, :] + grid - 1 == offsets[:, None, None]
    ).astype(jnp.bfloat16)


def pair_table(table, grid, offsets):
    heads = table.shape[1]
    side = 2 * grid - 1
    cells = grid * grid
    top = side * side
    inner = table[:top].reshape(side, side, heads)
    section = jnp.einsum(
        "rdh,dac->hrac", inner, offsets, preferred_element_type=jnp.float32
    ).astype(jnp.bfloat16)
    block = (
        jnp.einsum("hrac,rxy->hxayc", section, offsets, preferred_element_type=jnp.float32)
        .astype(jnp.bfloat16)
        .reshape(heads, cells, cells)
    )
    query_column = jnp.broadcast_to(table[top + 1][:, None, None], (heads, cells, 1))
    key_row = jnp.broadcast_to(table[top][:, None, None], (heads, 1, cells))
    corner = table[top + 2][:, None, None]
    upper = jnp.concatenate([block, query_column], axis=2)
    lower = jnp.concatenate([key_row, corner], axis=2)
    return jnp.concatenate([upper, lower], axis=1)


def cell_onehot(cells, lengths, rows, grid, keep):
    patch = (rows[None, :] >= 1) & (rows[None, :] < lengths[:, None])
    codes = jnp.where(patch, cells, grid * grid)
    slots = jnp.arange(grid * grid + 1, dtype=jnp.int32)
    onehot = (codes[:, :, None] == slots[None, None, :]) & keep[:, None, None]
    return onehot.astype(jnp.bfloat16)


def resolution_bias(table, grid, onehot_query, onehot_key):
    offsets = offset_table(grid)
    pairs = pair_table(table, grid, offsets)
    side_rows = jnp.einsum(
        "bqa,hac->bhqc", onehot_query, pairs, preferred_element_type=jnp.float32
    ).astype(jnp.bfloat16)
    return (
        jnp.einsum("bhqc,bkc->bhqk", side_rows, onehot_key, preferred_element_type=jnp.float32),
        offsets,
    )


def table_grad(d_scores, onehot_query, onehot_key, offsets, grid):
    highest = lax.Precision.HIGHEST
    heads = d_scores.shape[1]
    side = 2 * grid - 1
    cells = grid * grid
    keyside = jnp.einsum(
        "bhqk,bkc->bhqc", d_scores, onehot_key.astype(jnp.float32), precision=highest
    )
    pairs = jnp.einsum(
        "bqa,bhqc->hac", onehot_query.astype(jnp.float32), keyside, precision=highest
    )
    block = pairs[:, :cells, :cells].reshape(heads, grid, grid, grid, grid)
    weights = offsets.astype(jnp.float32)
    section = jnp.einsum("hxayc,rxy->hrac", block, weights, precision=highest)
    inner = jnp.einsum("hrac,dac->rdh", section, weights, precision=highest).reshape(
        side * side, heads
    )
    specials = jnp.stack(
        [
            jnp.sum(pairs[:, cells, :cells], axis=1),
            jnp.sum(pairs[:, :cells, cells], axis=1),
            pairs[:, cells, cells],
        ],
        axis=0,
    )
    return jnp.concatenate([inner, specials], axis=0)


def shards(
    tokens,
    resolution,
    positions,
    ln1_gain,
    ln1_bias,
    w_qkv,
    q_bias,
    v_bias,
    w_proj,
    proj_bias,
    gamma1,
    ln2_gain,
    ln2_bias,
    w_fc1,
    fc1_bias,
    w_fc2,
    fc2_bias,
    gamma2,
    rel_low,
    rel_high,
    grad_out,
):
    tokens_here, upstream_here = (tokens, grad_out)
    res_here, cells_here = (resolution, positions)
    first = lax.axis_index("blk") * tokens.shape[1]
    images, rows, width = tokens_here.shape
    heads = rel_low.shape[1]
    head_size = width // heads
    seq_len = positions.shape[1]
    scale = head_size ** (-0.5)
    count = images * rows
    high_flag = res_here == 1
    low_flag = jnp.logical_not(high_flag)
    grid = jnp.where(high_flag, G_HIGH, G_LOW).astype(jnp.int32)
    lengths = 1 + grid * grid
    own_rows = first + jnp.arange(rows, dtype=jnp.int32)
    all_rows = jnp.arange(seq_len, dtype=jnp.int32)
    own_cells = lax.dynamic_slice_in_dim(cells_here, first, rows, 1)
    everyone = jnp.ones_like(high_flag)
    query_low = cell_onehot(own_cells, lengths, own_rows, G_LOW, everyone)
    query_high = cell_onehot(own_cells, lengths, own_rows, G_HIGH, everyone)
    key_low = cell_onehot(cells_here, lengths, all_rows, G_LOW, low_flag)
    key_high = cell_onehot(cells_here, lengths, all_rows, G_HIGH, high_flag)
    bias_low, offsets_low = resolution_bias(rel_low, G_LOW, query_low, key_low)
    bias_high, offsets_high = resolution_bias(rel_high, G_HIGH, query_high, key_high)
    bias = bias_low + bias_high
    valid = (all_rows[None, :] < lengths[:, None])[:, None, None, :]
    gain1 = ln1_gain.astype(jnp.float32)
    gain2 = ln2_gain.astype(jnp.float32)
    scale1_layer = gamma1.astype(jnp.float32)
    scale2_layer = gamma2.astype(jnp.float32)
    inputs = tokens_here.reshape(count, width).astype(jnp.float32)
    normed1, factor1 = layer_stats(inputs)
    hidden1 = (normed1 * gain1 + ln1_bias.astype(jnp.float32)).astype(jnp.bfloat16)
    qkv_shift = jnp.concatenate([q_bias, jnp.zeros_like(q_bias), v_bias]).astype(jnp.float32)
    qkv = (
        (matmul(hidden1, w_qkv) + qkv_shift)
        .astype(jnp.bfloat16)
        .reshape(images, rows, 3, heads, head_size)
    )
    query = qkv[:, :, 0]
    keys_own = qkv[:, :, 1]
    values_own = qkv[:, :, 2]
    keys_all, values_all = (
        lax.all_gather(keys_own, "blk", axis=1, tiled=True),
        lax.all_gather(values_own, "blk", axis=1, tiled=True),
    )
    dots = (
        jnp.einsum("bqhd,bkhd->bhqk", query, keys_all, preferred_element_type=jnp.float32) * scale
        + bias
    )
    scores = jnp.where(valid, dots, -1e30)
    expo = jnp.exp(scores - jnp.max(scores, axis=-1, keepdims=True))
    probs = expo / jnp.sum(expo, axis=-1, keepdims=True)
    probs_low = probs.astype(jnp.bfloat16)
    mixed = (
        jnp.einsum("bhqk,bkhd->bqhd", probs_low, values_all, preferred_element_type=jnp.float32)
        .astype(jnp.bfloat16)
        .reshape(count, width)
    )
    attn = matmul(mixed, w_proj) + proj_bias.astype(jnp.float32)
    resid = inputs + scale1_layer * attn
    normed2, factor2 = layer_stats(resid)
    hidden2 = (normed2 * gain2 + ln2_bias.astype(jnp.float32)).astype(jnp.bfloat16)
    pre = matmul(hidden2, w_fc1) + fc1_bias.astype(jnp.float32)
    act = jax.nn.gelu(pre, approximate=False).astype(jnp.bfloat16)
    branch = matmul(act, w_fc2) + fc2_bias.astype(jnp.float32)
    output = (resid + scale2_layer * branch).reshape(images, rows, width).astype(jnp.bfloat16)
    upstream = upstream_here.reshape(count, width).astype(jnp.float32)
    d_gamma2 = jnp.sum(upstream * branch, axis=0)
    d_branch = (scale2_layer * upstream).astype(jnp.bfloat16)
    d_wfc2 = weight_grad(act, d_branch)
    d_fc2b = jnp.sum(d_branch.astype(jnp.float32), axis=0)
    d_pre = (matmul(d_branch, w_fc2.T) * gelu_slope(pre)).astype(jnp.bfloat16)
    d_wfc1 = weight_grad(hidden2, d_pre)
    d_fc1b = jnp.sum(d_pre.astype(jnp.float32), axis=0)
    d_hidden2 = matmul(d_pre, w_fc1.T)
    d_ln2g = jnp.sum(d_hidden2 * normed2, axis=0)
    d_ln2b = jnp.sum(d_hidden2, axis=0)
    d_resid = upstream + norm_back(d_hidden2, normed2, factor2, gain2)
    d_gamma1 = jnp.sum(d_resid * attn, axis=0)
    d_attn = (scale1_layer * d_resid).astype(jnp.bfloat16)
    d_wproj = weight_grad(mixed, d_attn)
    d_projb = jnp.sum(d_attn.astype(jnp.float32), axis=0)
    d_mixed = matmul(d_attn, w_proj.T).astype(jnp.bfloat16).reshape(images, rows, heads, head_size)
    d_probs = jnp.einsum("bqhd,bkhd->bhqk", d_mixed, values_all, preferred_element_type=jnp.float32)
    d_scores = probs * (d_probs - jnp.sum(probs * d_probs, axis=-1, keepdims=True))
    d_low = d_scores.astype(jnp.bfloat16)
    d_query = (
        jnp.einsum("bhqk,bkhd->bqhd", d_low, keys_all, preferred_element_type=jnp.float32) * scale
    )
    grad_low_table = table_grad(d_scores, query_low, key_low, offsets_low, G_LOW)
    grad_high_table = table_grad(d_scores, query_high, key_high, offsets_high, G_HIGH)
    d_table = jnp.concatenate([grad_low_table, grad_high_table], axis=0)
    low_size = grad_low_table.shape[0]
    size = rows * lax.axis_size("blk")
    d_key = jnp.einsum("bhqk,bqhd->kbhd", d_low, query, preferred_element_type=jnp.float32) * scale
    d_value = jnp.einsum("bhqk,bqhd->kbhd", probs_low, d_mixed, preferred_element_type=jnp.float32)
    kv_summed = lax.psum_scatter(
        jnp.concatenate(
            [d_key.reshape(size, images, width), d_value.reshape(size, images, width)], axis=2
        ).astype(jnp.bfloat16),
        "blk",
        scatter_dimension=0,
        tiled=True,
    )
    kv_round = kv_summed.transpose(1, 0, 2).reshape(count, 2 * width)
    d_qkv = jnp.concatenate([d_query.astype(jnp.bfloat16).reshape(count, width), kv_round], axis=1)
    d_wqkv = weight_grad(hidden1, d_qkv)
    d_columns = jnp.sum(d_qkv.astype(jnp.float32), axis=0)
    d_qb = d_columns[:width]
    d_vb = d_columns[2 * width :]
    d_hidden1 = matmul(d_qkv, w_qkv.T)
    d_ln1g = jnp.sum(d_hidden1 * normed1, axis=0)
    d_ln1b = jnp.sum(d_hidden1, axis=0)
    d_inputs = d_resid + norm_back(d_hidden1, normed1, factor1, gain1)
    grad_tokens = d_inputs.reshape(images, rows, width).astype(jnp.bfloat16)
    g_qkv, g_proj, g_fc1, g_fc2 = (
        lax.psum_scatter(d_wqkv, ("batch", "blk"), scatter_dimension=0, tiled=True),
        lax.psum_scatter(d_wproj, ("batch", "blk"), scatter_dimension=0, tiled=True),
        lax.psum_scatter(d_wfc1, ("batch", "blk"), scatter_dimension=0, tiled=True),
        lax.psum_scatter(d_wfc2, ("batch", "blk"), scatter_dimension=0, tiled=True),
    )
    (
        s_ln1g,
        s_ln1b,
        s_qb,
        s_vb,
        s_projb,
        s_gamma1,
        s_ln2g,
        s_ln2b,
        s_fc1b,
        s_fc2b,
        s_gamma2,
        s_table,
    ) = lax.psum(
        (
            d_ln1g,
            d_ln1b,
            d_qb,
            d_vb,
            d_projb,
            d_gamma1,
            d_ln2g,
            d_ln2b,
            d_fc1b,
            d_fc2b,
            d_gamma2,
            d_table,
        ),
        ("batch", "blk"),
    )
    return (
        output,
        grad_tokens,
        s_ln1g,
        s_ln1b,
        g_qkv,
        s_qb,
        s_vb,
        g_proj,
        s_projb,
        s_gamma1,
        s_ln2g,
        s_ln2b,
        g_fc1,
        s_fc1b,
        g_fc2,
        s_fc2b,
        s_gamma2,
        s_table[:low_size],
        s_table[low_size:],
    )


def solution(mesh):
    in_specs = (
        P("batch", "blk", None),
        P("batch"),
        P("batch", None),
        P(),
        P(),
        P(),
        P(),
        P(),
        P(),
        P(),
        P(),
        P(),
        P(),
        P(),
        P(),
        P(),
        P(),
        P(),
        P(),
        P(),
        P("batch", "blk", None),
    )
    out_specs = (
        P("batch", "blk", None),
        P("batch", "blk", None),
        P(),
        P(),
        P(("batch", "blk"), None),
        P(),
        P(),
        P(("batch", "blk"), None),
        P(),
        P(),
        P(),
        P(),
        P(("batch", "blk"), None),
        P(),
        P(("batch", "blk"), None),
        P(),
        P(),
        P(),
        P(),
    )
    return jax.shard_map(shards, mesh=mesh, in_specs=in_specs, out_specs=out_specs, check_vma=False)
```

profile of v0, /device:TPU:0, one launch (start us, length us, event | category | flops | bytes accessed | tf_op | source)
XLA Modules:
  0.0 1576.2 jit_solution(8320597050576733941)
XLA Ops:
  89.3 11.3 reshape.276
  100.6 19.7 %convert_bitcast_fusion = bf16[12,24,24,24,24]{4,3,2,0,1:T(8,128)(2,1)} fusion(bf16[47,47,12,1]{1,0,2,3:T(8,128)(2,1)} %reshape.301, s32[24,24]{1,0:T(8,128)S(1)} %subtract_add_fusion), kind=kOutput, calls=%fused_computation.1 | convolution fusion | flops 409140864 | bytes 8017944 | tf_op jit(solution)/shard_map/hrac,rxy->hxayc/dot_general | solution.py:59
  120.3 28.8 %copy.85 = bf16[12,24,24,24,24]{4,3,2,1,0:T(8,128)(2,1)} copy(bf16[12,24,24,24,24]{4,3,2,0,1:T(8,128)(2,1)} %convert_bitcast_fusion) | data formatting | bytes 15925248 | tf_op jit(solution)/shard_map/convert_element_type | solution.py:60
  149.1 48.4 %reshape.278 = bf16[12,576,576]{2,1,0:T(8,128)(2,1)} reshape(bf16[12,24,24,24,24]{4,3,2,1,0:T(8,128)(2,1)} %copy.85) | data formatting | bytes 15925248 | tf_op jit(solution)/shard_map/reshape | solution.py:61
  208.2 10.8 fusion.52
  219.0 13.5 copy.82
  232.6 12.1 fusion.55
  246.9 29.8 %add_select_fusion = f32[4,12,160,640]{3,2,1,0:T(8,128)} fusion(f32[4,12,160,640]{3,2,1,0:T(8,128)} %fusion.52, f32[4,12,160,640]{3,2,1,0:T(8,128)} %fusion.55, pred[4,640]{1,0:T(4,128)(4,1)S(1)} %copy-done.49, bf16[12,1,1]{2,1,0:T(2,128)(2,1)S(1)} %copy-done.44, bf16[12,1,576]{2,1,0:T(2,128)(2,1)} %broadcast_in_dim.65, ...), kind=kOutput, calls=%fused_computation.5 | convolution fusion | flops 10842352640 | bytes 68454936 | tf_op jit(solution)/shard_map/bhqc,bkc->bhqk/dot_general | solution.py:86
  276.7 21.2 %fusion.199 = (f32[4,12,160]{2,1,0:T(8,128)}, f32[4,12,160,640]{3,2,1,0:T(8,128)}) fusion(f32[4,12,160,640]{3,2,1,0:T(8,128)} %add_select_fusion), kind=kOutput, calls=%fused_computation.226 | output fusion | flops 9831039 | bytes 39352320 | tf_op jit(solution)/shard_map/sub | solution.py:192
  297.9 33.3 %all-gather.5.cloned.1.call-done = bf16[4,640,1,12,64]{4,0,3,2,1:T(4,128)(2,1)} async-done(((bf16[4,160,1,12,64]{4,0,3,2,1:T(4,128)(2,1)}), bf16[4,640,1,12,64]{4,0,3,2,1:T(4,128)(2,1)}) %all-gather.5.cloned.1.call-update) | async-done | bytes 3932176 | tf_op jit(solution)/shard_map/all_gather | solution.py:185
  331.2 13.5 copy.79
  344.7 28.5 %fusion.113 = bf16[4,160,12,64]{1,3,2,0:T(8,128)(2,1)} fusion(bf16[4,640,1,12,64]{1,4,3,0,2:T(8,128)(2,1)} %copy.79, f32[4,12,160]{2,1,0:T(8,128)} %get-tuple-element.65, f32[4,12,160,640]{3,2,1,0:T(8,128)} %add_select_fusion), kind=kOutput, calls=%fused_computation.137 | convolution fusion | flops 644391040 | bytes 24606720 | tf_op jit(solution)/shard_map/bhqk,bkhd->bqhd/dot_general | solution.py:196
  384.6 23.8 %fusion.25 = (bf16[640,3072]{1,0:T(8,128)(2,1)S(1)}, f32[640,3072]{1,0:T(8,128)}) fusion(f32[3072]{0:T(1024)S(1)} %copy-done.43, bf16[768,3072]{1,0:T(8,128)(2,1)} %param.34, f32[640,768]{1,0:T(8,128)S(1)} %get-tuple-element.49, f32[768]{0:T(1024)S(1)} %copy-done.22, f32[768]{0:T(1024)S(1)} %copy-done.20, f32[640]{0:T(1024)S(1)} %add_rsqrt_fusion, ...), kind=kOutput, calls=%fused_computation.28 | convolution fusion | flops 3152117760 | bytes 18504704 | tf_op jit(solution)/shard_map/dot_general | solution.py:33
  441.3 28.5 %fusion.69 = bf16[4,12,64,640]{3,2,1,0:T(8,128)(2,1)} fusion(bf16[4,160,12,64]{1,3,2,0:T(8,128)(2,1)} %copy.89, f32[4,12,160]{2,1,0:T(8,128)} %get-tuple-element.65, f32[4,12,160,640]{3,2,1,0:T(8,128)} %add_select_fusion), kind=kOutput, calls=%fused_computation.86 | convolution fusion | flops 645865600 | bytes 24606720 | tf_op jit(solution)/shard_map/bhqk,bqhd->kbhd/dot_general | solution.py:237
  476.1 17.0 %multiply_reduce_fusion = (f32[4,12,160]{2,1,0:T(8,128)S(1)}, f32[4,12,160,640]{3,2,1,0:T(8,128)}) fusion(f32[4,12,160,640]{3,2,1,0:T(8,128)} %get-tuple-element.66, f32[4,12,160]{2,1,0:T(8,128)} %get-tuple-element.65, bf16[4,160,12,64]{1,3,2,0:T(8,128)(2,1)} %copy.89, bf16[4,640,1,12,64]{1,4,3,0,2:T(8,128)(2,1)} %copy.79), kind=kOutput, calls=%fused_computation.3 | convolution fusion | flops 643883520 | bytes 44298240 | tf_op jit(solution)/shard_map/bqhd,bkhd->bhqk/dot_general | solution.py:225
  493.1 20.8 %subtract_multiply_fusion = f32[4,12,160,640]{3,2,1,0:T(8,128)} fusion(f32[4,12,160,640]{3,2,1,0:T(8,128)} %get-tuple-element.72, f32[4,12,160]{2,1,0:T(8,128)S(1)} %get-tuple-element.71, f32[4,12,160,640]{3,2,1,0:T(8,128)} %get-tuple-element.66, f32[4,12,160]{2,1,0:T(8,128)S(1)} %copy-done.16), kind=kLoop, calls=%fused_computation.2 | loop fusion | flops 14745600 | bytes 59043840 | tf_op jit(solution)/shard_map/mul | solution.py:226
  538.0 32.9 %fusion.1 = f32[4,12,160,577]{3,2,0,1:T(8,128)} fusion(f32[4,12,160,640]{3,2,1,0:T(8,128)} %subtract_multiply_fusion, s32[4,640]{1,0:T(4,128)S(1)} %copy-done.29, pred[4]{0:T(512)(128)(4,1)} %get-tuple-element.63), kind=kOutput, calls=%fused_computation.6 | convolution fusion | flops 34035798016 | bytes 37396484 | tf_op jit(solution)/shard_map/bhqk,bkc->bhqc/dot_general | solution.py:96
  570.9 31.3 %convolution_bitcast_fusion = f32[12,577,577]{1,2,0:T(8,128)S(1)} fusion(f32[4,12,160,577]{3,2,0,1:T(8,128)} %fusion.1, s32[4,160]{1,0:T(4,128)S(1)} %copy-done.48), kind=kOutput, calls=%fused_computation.25 | convolution fusion | flops 30683107328 | bytes 33708592 | tf_op jit(solution)/shard_map/bqa,bhqc->hac/dot_general | solution.py:99
  614.3 14.9 fusion.3
  646.3 12.9 reshape.285
  659.2 29.5 %copy.96 = f32[12,14,14,14,14]{3,4,1,2,0:T(8,128)} copy(f32[12,14,14,14,14]{2,1,4,3,0:T(8,128)} %reshape.285) | data formatting | bytes 3687936 | tf_op jit(solution)/shard_map/reshape | solution.py:102
  688.7 16.6 %convolution_bitcast_fusion.2 = f32[12,27,14,14]{1,3,2,0:T(8,128)S(1)} fusion(f32[12,14,14,14,14]{3,4,1,2,0:T(8,128)} %copy.96, s32[14,14]{1,0:T(8,128)S(1)} %copy-done.19), kind=kOutput, calls=%fused_computation.140 | convolution fusion | flops 149366704 | bytes 2098768 | tf_op jit(solution)/shard_map/hxayc,rxy->hrac/dot_general | solution.py:104
  710.1 52.1 %reshape.287 = f32[12,24,24,24,24]{2,1,4,3,0:T(8,128)} reshape(f32[12,576,576]{1,2,0:T(8,128)} %slice.101) | data formatting | bytes 31850496 | tf_op jit(solution)/shard_map/reshape | solution.py:102
  762.2 94.6 %copy.99 = f32[12,24,24,24,24]{3,4,1,2,0:T(8,128)} copy(f32[12,24,24,24,24]{2,1,4,3,0:T(8,128)} %reshape.287) | data formatting | bytes 31850496 | tf_op jit(solution)/shard_map/reshape | solution.py:102
  856.8 69.0 %fusion.164 = f32[47,12,24,24,1]{0,3,4,2,1:T(8,128)S(1)} fusion(f32[12,24,24,24,24]{3,4,1,2,0:T(8,128)} %copy.99, s32[24,24]{1,0:T(8,128)S(1)} %copy-done.13), kind=kOutput, calls=%fused_computation.171 | convolution fusion | flops 2245487104 | bytes 17227008 | tf_op jit(solution)/shard_map/hxayc,rxy->hrac/dot_general | solution.py:104
  958.8 13.0 fusion.118
  991.5 63.5 %all-reduce.3.cloned.1.call-done = f32[2944,12]{0,1:T(8,128)} async-done(((f32[2944,12]{0,1:T(8,128)}), f32[2944,12]{0,1:T(8,128)}) %all-reduce.3.cloned.1.call-update) | async-done | bytes 141328 | tf_op jit(solution)/shard_map/psum | solution.py:276
  1067.8 42.9 %all-reduce = (f32[768]{0:T(1024)}, f32[768]{0:T(1024)}, f32[768]{0:T(1024)}, f32[768]{0:T(1024)}, f32[768]{0:T(1024)}, /*index=5*/f32[768]{0:T(1024)}, f32[768]...) all-reduce(f32[768]{0:T(1024)} %get-tuple-element.21, ...), channel_id=1, replica_groups=mesh['batch'=8,'blk'=4] {'batch','blk'}, use_global_device_ids=true, to_apply=%region_13.14 | all-reduce | flops 10752 | bytes 86016 | tf_op jit(solution)/shard_map/psum | solution.py:276
  1116.1 44.6 %reduce-scatter.10.cloned.1.call-done = f32[24,768]{1,0:T(8,128)} async-done(((f32[768,768]{1,0:T(8,128)}), f32[24,768]{1,0:T(8,128)}) %reduce-scatter.10.cloned.1.call-update) | async-done | bytes 73744 | tf_op jit(solution)/shard_map/reduce_scatter | solution.py:259
  1160.6 141.9 %reduce-scatter.12.cloned.1.call-done = f32[24,3072]{1,0:T(8,128)} async-done(((f32[768,3072]{1,0:T(8,128)}), f32[24,3072]{1,0:T(8,128)}) %reduce-scatter.12.cloned.1.call-update) | async-done | bytes 294928 | tf_op jit(solution)/shard_map/reduce_scatter | solution.py:260
  1302.5 141.3 %reduce-scatter.14.cloned.1.call-done = f32[96,768]{1,0:T(8,128)} async-done(((f32[3072,768]{1,0:T(8,128)}), f32[96,768]{1,0:T(8,128)}) %reduce-scatter.14.cloned.1.call-update) | async-done | bytes 294928 | tf_op jit(solution)/shard_map/reduce_scatter | solution.py:261
  1443.7 125.4 %reduce-scatter.8.cloned.1.call-done = f32[24,2304]{1,0:T(8,128)} async-done(((f32[768,2304]{1,0:T(8,128)}), f32[24,2304]{1,0:T(8,128)}) %reduce-scatter.8.cloned.1.call-update) | async-done | bytes 221200 | tf_op jit(solution)/shard_map/reduce_scatter | solution.py:258
  (238 shorter events, 274.1 us)
Async XLA Ops:
  7.2 211.8 %all-gather.7.cloned.1.call-start = ((), (), s32[]{:S(2)}) async-start(), calls=%async_computation.12 | async-start | bytes 9830400 | tf_op jit(solution)/shard_map/all_gather | solution.py:184
  46.3 284.8 %all-gather.5.cloned.1.call-start = ((), (), s32[]{:S(2)}) async-start(), calls=%async_computation.11 | async-start | bytes 9830400 | tf_op jit(solution)/shard_map/all_gather | solution.py:185
  51.9 928.9 %reduce-scatter.6.cloned.1.call-start = ((), (), s32[]{:S(2)}) async-start(), calls=%async_computation.5 | async-start | bytes 9830400 | tf_op jit(solution)/shard_map/reduce_scatter | solution.py:238
  55.0 45.6 %copy-start.12 = (s32[24,24]{1,0:T(8,128)}, s32[24,24]{1,0:T(8,128)S(1)}, u32[]{:S(2)}) copy-start(s32[24,24]{1,0:T(8,128)S(1)} %subtract_add_fusion) | copy-start | bytes 6916
  60.7 137.6 %copy-start.36 = (f32[768]{0:T(1024)}, f32[768]{0:T(1024)S(1)}, u32[]{:S(2)}) copy-start(f32[768]{0:T(1024)S(1)} %convert_element_type.197) | copy-start | bytes 9220
  198.3 20.6 %copy-start.14 = (s32[4,640]{1,0:T(4,128)}, s32[4,640]{1,0:T(4,128)S(1)}, u32[]{:S(2)}) copy-start(s32[4,640]{1,0:T(4,128)S(1)} %get-tuple-element.62) | copy-start | bytes 30724
  205.2 13.8 copy-start.26
  232.6 14.3 copy-start.44
  232.6 14.3 copy-start.47
  232.6 14.3 copy-start.49
  380.9 27.5 %slice-start.2 = ((s8[4718592]{0:T(1024)(128)(4,1)}), s8[4194304]{0:T(1024)(128)(4,1)S(1)}, s32[]{:S(2)}) async-start(s8[4718592]{0:T(1024)(128)(4,1)} %bitcast.305), calls=%async_computation.15 | async-start | bytes 8388608
  381.0 36.9 %slice-start = ((s8[4718592]{0:T(1024)(128)(4,1)}), s8[4194304]{0:T(1024)(128)(4,1)S(1)}, s32[]{:S(2)}) async-start(s8[4718592]{0:T(1024)(128)(4,1)} %bitcast.303), calls=%async_computation.13 | async-start | bytes 8388608
  384.2 37.9 %copy-start.3 = (f32[640,768]{1,0:T(8,128)}, f32[640,768]{1,0:T(8,128)S(1)}, u32[]{:S(2)}) copy-start(f32[640,768]{1,0:T(8,128)S(1)} %get-tuple-element.49) | copy-start | bytes 5898244
  384.2 37.9 %copy-start.17 = (f32[640]{0:T(1024)}, f32[640]{0:T(1024)S(1)}, u32[]{:S(2)}) copy-start(f32[640]{0:T(1024)S(1)} %broadcast_multiply_fusion.4) | copy-start | bytes 7684
  384.6 37.5 %copy-start.24 = (f32[640]{0:T(1024)}, f32[640]{0:T(1024)S(1)}, u32[]{:S(2)}) copy-start(f32[640]{0:T(1024)S(1)} %add_rsqrt_fusion) | copy-start | bytes 7684
  384.6 23.9 %copy-start.10 = (bf16[640,768]{1,0:T(8,128)(2,1)S(1)}, bf16[640,768]{1,0:T(8,128)(2,1)}, u32[]{:S(2)}) copy-start(bf16[640,768]{1,0:T(8,128)(2,1)} %fusion.80) | copy-start | bytes 2949124
  384.6 23.9 %slice-start.3 = ((s8[4718592]{0:T(1024)(128)(4,1)}), s8[524288]{0:T(1024)(128)(4,1)S(1)}, s32[]{:S(2)}) async-start(s8[4718592]{0:T(1024)(128)(4,1)} %bitcast.305), calls=%async_computation.16 | async-start | bytes 1048576
  384.6 33.2 %slice-start.1 = ((s8[4718592]{0:T(1024)(128)(4,1)}), s8[524288]{0:T(1024)(128)(4,1)S(1)}, s32[]{:S(2)}) async-start(s8[4718592]{0:T(1024)(128)(4,1)} %bitcast.303), calls=%async_computation.14 | async-start | bytes 1048576
  476.1 17.0 %copy-start.16 = (f32[4,12,160]{2,1,0:T(8,128)S(1)}, f32[4,12,160]{2,1,0:T(8,128)}, u32[]{:S(2)}) copy-start(f32[4,12,160]{2,1,0:T(8,128)} %get-tuple-element.65) | copy-start | bytes 92164
  493.1 20.8 %copy-start.2 = (bf16[4,160,1,12,64]{1,0,4,3,2:T(4,128)(2,1)S(1)}, bf16[4,160,1,12,64]{1,0,4,3,2:T(4,128)(2,1)}, u32[]{:S(2)}) copy-start(bf16[4,160,1,12,64]{1,0,4,3,2:T(4,128)(2,1)} %get-tuple-element.50) | copy-start | bytes 2949124
  537.4 33.5 %copy-start.48 = (s32[4,160]{1,0:T(4,128)S(1)}, s32[4,160]{1,0:T(4,128)}, u32[]{:S(2)}) copy-start(s32[4,160]{1,0:T(4,128)} %get-tuple-element.59) | copy-start | bytes 7684
  537.4 517.6 %all-reduce.3.cloned.1.call-start = ((), (), s32[]{:S(2)}) async-start(), calls=%async_computation.10 | async-start | bytes 376832 | tf_op jit(solution)/shard_map/psum | solution.py:276
  614.3 14.9 copy-start.27
  659.2 29.5 %copy-start.19 = (s32[14,14]{1,0:T(8,128)S(1)}, s32[14,14]{1,0:T(8,128)}, u32[]{:S(2)}) copy-start(s32[14,14]{1,0:T(8,128)} %subtract_add_fusion.1) | copy-start | bytes 2356
  762.2 94.6 %copy-start.13 = (s32[24,24]{1,0:T(8,128)S(1)}, s32[24,24]{1,0:T(8,128)}, u32[]{:S(2)}) copy-start(s32[24,24]{1,0:T(8,128)} %copy-done.12) | copy-start | bytes 6916
  933.7 226.9 %reduce-scatter.10.cloned.1.call-start = ((), (), s32[]{:S(2)}) async-start(), calls=%async_computation.7 | async-start | bytes 2433024 | tf_op jit(solution)/shard_map/reduce_scatter | solution.py:259
  938.0 364.5 %reduce-scatter.12.cloned.1.call-start = ((), (), s32[]{:S(2)}) async-start(), calls=%async_computation.8 | async-start | bytes 9732096 | tf_op jit(solution)/shard_map/reduce_scatter | solution.py:260
  948.5 495.2 %reduce-scatter.14.cloned.1.call-start = ((), (), s32[]{:S(2)}) async-start(), calls=%async_computation.9 | async-start | bytes 9732096 | tf_op jit(solution)/shard_map/reduce_scatter | solution.py:261
  958.5 610.6 %reduce-scatter.8.cloned.1.call-start = ((), (), s32[]{:S(2)}) async-start(), calls=%async_computation.6 | async-start | bytes 7299072 | tf_op jit(solution)/shard_map/reduce_scatter | solution.py:258
  989.4 71.6 %copy-start.31 = (f32[640]{0:T(1024)S(1)}, f32[640]{0:T(1024)}, u32[]{:S(2)}) copy-start(f32[640]{0:T(1024)} %copy-done.30) | copy-start | bytes 7684
  989.4 71.6 %copy-start.33 = (f32[768]{0:T(1024)S(1)}, f32[768]{0:T(1024)}, u32[]{:S(2)}) copy-start(f32[768]{0:T(1024)} %copy-done.32) | copy-start | bytes 9220
  989.4 71.6 %copy-start.35 = (f32[640]{0:T(1024)S(1)}, f32[640]{0:T(1024)}, u32[]{:S(2)}) copy-start(f32[640]{0:T(1024)} %copy-done.34) | copy-start | bytes 7684
  (34 other events, 209.0 us)
Sparse Core Ops, SparseCore 0:
  46.5 143.7 all-gather.6
  191.8 139.2 all-gather.4
  537.5 134.4 reduce-scatter.5
  933.8 121.1 all-reduce.2
  1060.7 99.8 reduce-scatter.9
  1168.0 134.4 reduce-scatter.11
  1309.0 134.7 reduce-scatter.13
  1450.9 118.1 reduce-scatter.7
where the time goes:
time: 1590 us; the launch traced here: 1580 us
  waiting for transfers between devices  550 us (35%)
  matrix products  444 us (28%)
  local copies, waits for them, and re-layouts  431 us (27%)
  other arithmetic  92.9 us (6%)
  blocking collectives  42.9 us (3%)
    reshape x4, local copies, waits for them, and re-layouts, table_grad(): block = pairs[:, :cells, :cells].reshape(heads, grid, grid, grid, grid)  189 us
    reduce_scatter x1, waiting for transfers between devices, shards(): lax.psum_scatter(d_wfc1, ('batch', 'blk'), scatter_dimension=0, tiled=True)  142 us
    reduce_scatter x1, waiting for transfers between devices, shards(): lax.psum_scatter(d_wfc2, ('batch', 'blk'), scatter_dimension=0, tiled=True)  141 us
    reduce_scatter x1, waiting for transfers between devices, shards(): lax.psum_scatter(d_wqkv, ('batch', 'blk'), scatter_dimension=0, tiled=True)  125 us
    dot_general x2, matrix products, table_grad(): section = jnp.einsum('hxayc,rxy->hrac', block, weights, precision=highest)  85.7 us
    psum x1, waiting for transfers between devices, shards(): lax.psum((d_ln1g, d_ln1b, d_qb, d_vb, d_projb, d_gamma1, d_ln2g, d_ln2b,...  63.5 us
    reshape x2, local copies, waits for them, and re-layouts, pair_table(): block = jnp.einsum('hrac,rxy->hxayc', section, offsets, preferred_element...  59.6 us
    dot_general x8, matrix products, matmul(): return jnp.dot(left, right, preferred_element_type=jnp.float32)  58.7 us
  transfers between devices with their start and end apart: 8, of which 6 were waited for; matrix products, arithmetic and copies ran while one was open for 45% of the time, Pallas kernels for 0%

commit v1 on v0

v1 whole, which is shorter than its diff:
```python
import functools

import jax
import jax.numpy as jnp
import numpy as np
from jax import lax
from jax.experimental import pallas as pl
from jax.experimental.pallas import tpu as pltpu
from jax.sharding import PartitionSpec as P

G_LOW = 14
G_HIGH = 24
SIDE_LOW = 2 * G_LOW - 1
SIDE = 2 * G_HIGH - 1
CELLS = G_HIGH * G_HIGH
SPAN = 1152
F32 = jnp.float32
BF16 = jnp.bfloat16


def layer_stats(values):
    center = values - jnp.mean(values, axis=-1, keepdims=True)
    factor = lax.rsqrt(jnp.mean(center * center, axis=-1, keepdims=True) + 1e-06)
    return (center * factor, factor)


def norm_back(grad, normed, factor, gain):
    scaled = grad * gain
    return factor * (
        scaled
        - jnp.mean(scaled, axis=-1, keepdims=True)
        - normed * jnp.mean(scaled * normed, axis=-1, keepdims=True)
    )


def gelu_slope(values):
    return (
        0.5 * (1.0 + lax.erf(values * 0.7071067811865476))
        + values * jnp.exp(-0.5 * values * values) * 0.3989422804014327
    )


def matmul(left, right):
    return jnp.dot(left, right, preferred_element_type=F32)


def matmul_t(left, right):
    return lax.dot_general(left, right, (((1,), (1,)), ((), ())), preferred_element_type=F32)


def t_matmul(left, right):
    return lax.dot_general(left, right, (((0,), (0,)), ((), ())), preferred_element_type=F32)


def slot_tables(seq):
    tokens = np.arange(seq)
    tables = []
    for grid in (G_LOW, G_HIGH):
        cells = np.arange(CELLS)
        used = (cells // G_HIGH < grid) & (cells % G_HIGH < grid)
        free = np.concatenate([cells[~used], np.arange(CELLS + 1, seq)])
        slot = np.full(seq, CELLS)
        slot[1 + grid * grid :] = free
        patch = np.concatenate([used, np.zeros(seq - CELLS, bool)])
        key = patch.copy()
        key[CELLS] = True
        tables.append((slot, (tokens >= 1) & (tokens < 1 + grid * grid), patch, key))
    return [np.stack(parts) for parts in zip(*tables)]


def lane_tables():
    lanes = np.arange(SPAN)
    spread = (lanes[None, :] // G_HIGH == np.arange(128)[:, None]) & (np.arange(128)[:, None] < SIDE)
    code = np.arange(48)[:, None] + (lanes % G_HIGH)[None, :]
    return spread, code.astype(np.int32)


def bias_kernel(special, table, spread, code, patch, mask, out, wide, full):
    head = pl.program_id(0)
    flat = matmul(table[0], spread[...])
    codes = code[...]
    for a in range(G_HIGH):
        picked = jnp.where(codes == a + G_HIGH - 1, flat, 0.0)
        wide[a : a + 1, :] = jnp.sum(picked, axis=0, keepdims=True)
    for r in range(G_HIGH):
        at = (G_HIGH - 1 - r) * G_HIGH
        full[r * G_HIGH : (r + 1) * G_HIGH, 0:CELLS] = wide[:, at : at + CELLS]
    seq = full.shape[0]
    column = lax.broadcasted_iota(jnp.int32, (1, seq), 1)
    inner_row = jnp.where(column < CELLS, special[head, 0], special[head, 2])
    values = jnp.where(column < CELLS, full[...], special[head, 1])
    values = jnp.where(patch[...] > 0.0, values, inner_row)
    out[0] = (values + mask[...]).astype(BF16)


def make_bias(table, special, spread, code, patch, mask):
    heads, seq = table.shape[0], patch.shape[0]
    whole = lambda shape: pl.BlockSpec(shape, lambda h: (0,) * len(shape))
    return pl.pallas_call(
        bias_kernel,
        grid=(heads,),
        out_shape=jax.ShapeDtypeStruct((heads, seq, seq), BF16),
        in_specs=[
            pl.BlockSpec(memory_space=pltpu.SMEM),
            pl.BlockSpec((1, 48, 128), lambda h: (h, 0, 0)),
            whole(spread.shape),
            whole(code.shape),
            whole(patch.shape),
            whole(mask.shape),
        ],
        out_specs=pl.BlockSpec((1, seq, seq), lambda h: (h, 0, 0)),
        scratch_shapes=[pltpu.VMEM((G_HIGH, SPAN), F32), pltpu.VMEM((seq, seq), F32)],
        compiler_params=pltpu.CompilerParams(vmem_limit_bytes=48 << 20),
        name="bias",
    )(special, table, spread, code, patch, mask)


FWD_ROWS = 128


def forward_kernel(query, keys, values, bias, probs, mixed):
    seq = query.shape[0]
    for h in range(2):
        at = slice(h * 64, h * 64 + 64)
        k = keys[:, at]
        v = values[:, at]
        for r in range(0, seq, FWD_ROWS):
            rows = slice(r, r + FWD_ROWS)
            scores = matmul_t(query[rows, at] * 0.125, k) + bias[h, rows, :].astype(F32)
            expo = jnp.exp(scores - jnp.max(scores, axis=-1, keepdims=True))
            low = (expo / jnp.sum(expo, axis=-1, keepdims=True)).astype(BF16)
            probs[h, rows, :] = low
            mixed[rows, at] = matmul(low, v).astype(BF16)


def attention(qkv, bias):
    seq = qkv.shape[0]
    width = qkv.shape[1] // 3
    pairs = width // 128
    column = lambda part: pl.BlockSpec((seq, 128), lambda h: (0, part * pairs + h))
    square = pl.BlockSpec((2, seq, seq), lambda h: (h, 0, 0))
    return pl.pallas_call(
        forward_kernel,
        grid=(pairs,),
        out_shape=(
            jax.ShapeDtypeStruct((2 * pairs, seq, seq), BF16),
            jax.ShapeDtypeStruct((seq, width), BF16),
        ),
        in_specs=[column(0), column(1), column(2), square],
        out_specs=(square, column(0)),
        compiler_params=pltpu.CompilerParams(vmem_limit_bytes=48 << 20),
        name="attention",
    )(qkv, qkv, qkv, bias)


def backward_kernel(query, keys, values, probs, upstream, patch, spread, code, d_query, d_key, d_value, d_table, d_edge, score, wide):
    seq = query.shape[0]
    step = 128
    for h in range(2):
        at = slice(h * 64, h * 64 + 64)
        k = keys[:, at]
        v = values[:, at]
        dk = jnp.zeros((seq, 64), F32)
        dv = jnp.zeros((seq, 64), F32)
        for r in range(0, seq, step):
            rows = slice(r, r + step)
            low = probs[h, rows, :]
            up = upstream[rows, at]
            weight = low.astype(F32)
            product = weight * matmul_t(up, v)
            ds = product - weight * jnp.sum(product, axis=-1, keepdims=True)
            score[rows, :] = ds
            ds_low = ds.astype(BF16)
            d_query[rows, at] = (matmul(ds_low, k) * 0.125).astype(BF16)
            dk += t_matmul(ds_low, query[rows, at] * 0.125)
            dv += t_matmul(low, up)
        d_key[:, at] = dk.astype(BF16)
        d_value[:, at] = dv.astype(BF16)
        wide[...] = jnp.zeros_like(wide)
        inside = jnp.zeros((1, seq), F32)
        total = jnp.zeros((1, seq), F32)
        for r in range(0, seq, 128):
            rows = slice(r, r + 128)
            ds = score[rows, :]
            total += jnp.sum(ds, axis=0, keepdims=True)
            ds = ds * patch[rows, :]
            inside += jnp.sum(ds, axis=0, keepdims=True)
        for r in range(G_HIGH):
            rows = slice(r * G_HIGH, (r + 1) * G_HIGH)
            off = (G_HIGH - 1 - r) * G_HIGH
            wide[:, off : off + CELLS] += score[rows, 0:CELLS] * patch[rows, :]
        d_edge[h, 0:1, :] = inside
        d_edge[h, 1:2, :] = total - inside
        codes = code[...]
        flat = jnp.zeros((48, SPAN), F32)
        for a in range(G_HIGH):
            flat += jnp.where(codes == a + G_HIGH - 1, wide[a : a + 1, :], 0.0)
        high = flat.astype(BF16)
        rest = flat - high.astype(F32)
        middle = rest.astype(BF16)
        last = (rest - middle.astype(F32)).astype(BF16)
        d_table[h] = matmul_t(high, spread[...]) + matmul_t(middle, spread[...]) + matmul_t(last, spread[...])


def attention_back(qkv, probs, upstream, patch, spread, code):
    seq = qkv.shape[0]
    width = qkv.shape[1] // 3
    pairs = width // 128
    column = lambda part: pl.BlockSpec((seq, 128), lambda h: (0, part * pairs + h))
    whole = lambda shape: pl.BlockSpec(shape, lambda h: (0,) * len(shape))
    flat = jax.ShapeDtypeStruct((seq, width), BF16)
    return pl.pallas_call(
        backward_kernel,
        grid=(pairs,),
        out_shape=(
            flat,
            flat,
            flat,
            jax.ShapeDtypeStruct((2 * pairs, 48, 128), F32),
            jax.ShapeDtypeStruct((2 * pairs, 8, seq), F32),
        ),
        in_specs=[
            column(0),
            column(1),
            column(2),
            pl.BlockSpec((2, seq, seq), lambda h: (h, 0, 0)),
            column(0),
            whole(patch.shape),
            whole(spread.shape),
            whole(code.shape),
        ],
        out_specs=(
            column(0),
            column(0),
            column(0),
            pl.BlockSpec((2, 48, 128), lambda h: (h, 0, 0)),
            pl.BlockSpec((2, 8, seq), lambda h: (h, 0, 0)),
        ),
        scratch_shapes=[pltpu.VMEM((seq, seq), F32), pltpu.VMEM((G_HIGH, SPAN), F32)],
        compiler_params=pltpu.CompilerParams(vmem_limit_bytes=48 << 20),
        name="attention_back",
    )(qkv, qkv, qkv, probs, upstream, patch, spread, code)


def exchange(blocks, count, me):
    result = jnp.zeros_like(blocks)
    result = lax.dynamic_update_index_in_dim(
        result, lax.dynamic_index_in_dim(blocks, me, 0, keepdims=False), me, 0
    )
    for shift in range(1, count):
        there = lax.rem(me + shift, count)
        back = lax.rem(me + count - shift, count)
        part = lax.ppermute(
            lax.dynamic_index_in_dim(blocks, there, 0, keepdims=False),
            "blk",
            [(i, (i + shift) % count) for i in range(count)],
        )
        result = lax.dynamic_update_index_in_dim(result, part, back, 0)
    return result


def swap(value, axis, bit, count):
    return lax.ppermute(value, axis, [(i, i ^ bit) for i in range(count)])


def bits_of(count):
    return [1 << i for i in range(count.bit_length() - 1)]


def scatter_sum(grad, batch, blk, flip):
    places = [("batch", bit, batch) for bit in bits_of(batch)][::-1]
    places += [("blk", bit, blk) for bit in bits_of(blk)][::-1]
    value = grad.reshape((2,) * len(places) + (grad.shape[0] >> len(places), grad.shape[1]))
    order = [p for p in places if p[0] == "batch"][::-1] + [p for p in places if p[0] == "blk"][::-1]
    if flip:
        order = order[:1] + order[1 : len(bits_of(batch))][::-1] + order[len(bits_of(batch)) :]
    left = list(places)
    for place in order:
        axis, bit, count = place
        at = left.index(place)
        left.remove(place)
        mine = jnp.bitwise_and(lax.axis_index(axis) // bit, 1)
        sent = lax.dynamic_index_in_dim(value, 1 - mine, at, keepdims=False)
        kept = lax.dynamic_index_in_dim(value, mine, at, keepdims=False)
        got = swap(sent, axis, bit, count)
        value = kept.astype(F32) + got.astype(F32)
        if left:
            value = value.astype(BF16)
    return value


def total_sum(value, batch, blk):
    for bit in bits_of(batch):
        value = value + swap(value, "batch", bit, batch)
    for bit in bits_of(blk):
        value = value + swap(value, "blk", bit, blk)
    return value


def packed(parts):
    flat = jnp.concatenate([p.reshape(-1) for p in parts])
    size = flat.shape[0]
    rows = -(-size // 1024) * 8
    return jnp.pad(flat, (0, rows * 128 - size)).reshape(rows, 128)


def unpacked(value, shapes):
    flat = value.reshape(-1)
    result, at = [], 0
    for shape in shapes:
        size = int(np.prod(shape))
        result.append(flat[at : at + size].reshape(shape))
        at += size
    return result


def shards(
    batch,
    blk,
    tokens,
    resolution,
    positions,
    ln1_gain,
    ln1_bias,
    w_qkv,
    q_bias,
    v_bias,
    w_proj,
    proj_bias,
    gamma1,
    ln2_gain,
    ln2_bias,
    w_fc1,
    fc1_bias,
    w_fc2,
    fc2_bias,
    gamma2,
    rel_low,
    rel_high,
    grad_out,
):
    images, rows, width = tokens.shape
    seq = positions.shape[1]
    heads = rel_low.shape[1]
    assert images == blk and rows * blk == seq and width == heads * 64
    me = lax.axis_index("blk")

    slot_np, token_np, patch_np, key_np = slot_tables(seq)
    high = lax.dynamic_index_in_dim(resolution, me, 0, keepdims=False) == 1
    cells = lax.dynamic_index_in_dim(positions, me, 0, keepdims=False)
    grid = jnp.where(high, G_HIGH, G_LOW)
    pick = lambda pair: jnp.where(high, pair[1], pair[0])
    slot = jnp.where(pick(token_np), (cells // grid) * G_HIGH + cells % grid, pick(slot_np))
    patch = pick(patch_np).astype(F32)[:, None]
    mask = jnp.where(pick(key_np), 0.0, -1e30).astype(F32)[None, :]
    slots = jnp.arange(seq, dtype=jnp.int32)
    to_slot = (slots[:, None] == slot[None, :]).astype(BF16)
    to_token = (slots[None, :] == slot[:, None]).astype(BF16)

    pad = G_HIGH - G_LOW
    top_low, top_high = SIDE_LOW * SIDE_LOW, SIDE * SIDE
    inner_low = jnp.pad(
        rel_low[:top_low].T.reshape(heads, SIDE_LOW, SIDE_LOW), ((0, 0), (pad, pad), (pad, pad))
    )
    inner_high = rel_high[:top_high].T.reshape(heads, SIDE, SIDE)
    inner = jnp.where(high, inner_high, inner_low)[:, ::-1, :].transpose(0, 2, 1)
    table = jnp.pad(inner, ((0, 0), (0, 48 - SIDE), (0, 128 - SIDE)))
    special = jnp.where(high, rel_high[top_high:], rel_low[top_low:]).T.astype(F32)
    spread_np, code_np = lane_tables()
    spread = jnp.asarray(spread_np, BF16)
    code = jnp.asarray(code_np)
    bias = make_bias(table, special, spread, code, patch, mask)

    raw = exchange(tokens, blk, me).reshape(seq, width)
    inputs = matmul(to_slot, raw)
    raw_up = exchange(grad_out, blk, me).reshape(seq, width)

    gain1 = ln1_gain.astype(F32)
    gain2 = ln2_gain.astype(F32)
    scale1_layer = gamma1.astype(F32)
    scale2_layer = gamma2.astype(F32)
    normed1, factor1 = layer_stats(inputs)
    hidden1 = (normed1 * gain1 + ln1_bias.astype(F32)).astype(BF16)
    qkv_shift = jnp.concatenate([q_bias, jnp.zeros_like(q_bias), v_bias]).astype(F32)
    qkv = (matmul(hidden1, w_qkv) + qkv_shift).astype(BF16)
    probs, mixed = attention(qkv, bias)
    attn = matmul(mixed, w_proj) + proj_bias.astype(F32)
    resid = inputs + scale1_layer * attn
    normed2, factor2 = layer_stats(resid)
    hidden2 = (normed2 * gain2 + ln2_bias.astype(F32)).astype(BF16)
    pre = matmul(hidden2, w_fc1) + fc1_bias.astype(F32)
    act = jax.nn.gelu(pre, approximate=False).astype(BF16)
    branch = matmul(act, w_fc2) + fc2_bias.astype(F32)
    out_slot = (resid + scale2_layer * branch).astype(BF16)
    output = exchange(matmul(to_token, out_slot).astype(BF16).reshape(blk, rows, width), blk, me)

    upstream = matmul(to_slot, raw_up)
    d_gamma2 = jnp.sum(upstream * branch, axis=0)
    d_branch = (scale2_layer * upstream).astype(BF16)
    g_fc2 = scatter_sum(t_matmul(act, d_branch).astype(BF16), batch, blk, False)
    d_fc2b = jnp.sum(d_branch.astype(F32), axis=0)
    d_pre = (matmul_t(d_branch, w_fc2) * gelu_slope(pre)).astype(BF16)
    g_fc1 = scatter_sum(t_matmul(hidden2, d_pre).astype(BF16), batch, blk, True)
    d_fc1b = jnp.sum(d_pre.astype(F32), axis=0)
    d_hidden2 = matmul_t(d_pre, w_fc1)
    d_ln2g = jnp.sum(d_hidden2 * normed2, axis=0)
    d_ln2b = jnp.sum(d_hidden2, axis=0)
    d_resid = upstream + norm_back(d_hidden2, normed2, factor2, gain2)
    d_gamma1 = jnp.sum(d_resid * attn, axis=0)
    d_attn = (scale1_layer * d_resid).astype(BF16)
    g_proj = scatter_sum(t_matmul(mixed, d_attn).astype(BF16), batch, blk, False)
    d_projb = jnp.sum(d_attn.astype(F32), axis=0)
    d_mixed = matmul_t(d_attn, w_proj).astype(BF16)
    early = [d_gamma2, d_fc2b, d_fc1b, d_ln2g, d_ln2b, d_gamma1, d_projb]
    early_sum = total_sum(packed(early), batch, blk)

    d_query, d_key, d_value, d_table, d_edge = attention_back(qkv, probs, d_mixed, patch, spread, code)
    d_qkv = jnp.concatenate([d_query, d_key, d_value], axis=1)
    g_qkv = scatter_sum(t_matmul(hidden1, d_qkv).astype(BF16), batch, blk, True)
    d_qb = jnp.sum(d_query.astype(F32), axis=0)
    d_vb = jnp.sum(d_value.astype(F32), axis=0)
    d_hidden1 = matmul_t(d_qkv, w_qkv)
    d_ln1g = jnp.sum(d_hidden1 * normed1, axis=0)
    d_ln1b = jnp.sum(d_hidden1, axis=0)
    d_inputs = (d_resid + norm_back(d_hidden1, normed1, factor1, gain1)).astype(BF16)
    grad_tokens = exchange(matmul(to_token, d_inputs).astype(BF16).reshape(blk, rows, width), blk, me)

    offsets = d_table[:, :SIDE, :SIDE].transpose(0, 2, 1)[:, ::-1, :]
    tops = jnp.stack(
        [jnp.sum(d_edge[:, 1, :CELLS], axis=1), d_edge[:, 0, CELLS], d_edge[:, 1, CELLS]], axis=1
    )
    high_grad = jnp.concatenate([offsets.reshape(heads, top_high), tops], axis=1)
    small = offsets[:, pad : pad + SIDE_LOW, pad : pad + SIDE_LOW]
    low_grad = jnp.concatenate([small.reshape(heads, top_low), tops], axis=1)
    high_grad = jnp.where(high, high_grad, 0.0)
    low_grad = jnp.where(high, 0.0, low_grad)
    late = [d_ln1g, d_ln1b, d_qb, d_vb, low_grad, high_grad]
    late_sum = total_sum(packed(late), batch, blk)

    s_gamma2, s_fc2b, s_fc1b, s_ln2g, s_ln2b, s_gamma1, s_projb = unpacked(
        early_sum, [p.shape for p in early]
    )
    s_ln1g, s_ln1b, s_qb, s_vb, s_low, s_high = unpacked(late_sum, [p.shape for p in late])
    return (
        output,
        grad_tokens,
        s_ln1g,
        s_ln1b,
        g_qkv,
        s_qb,
        s_vb,
        g_proj,
        s_projb,
        s_gamma1,
        s_ln2g,
        s_ln2b,
        g_fc1,
        s_fc1b,
        g_fc2,
        s_fc2b,
        s_gamma2,
        s_low.T,
        s_high.T,
    )


def solution(mesh):
    rows = P("batch", "blk", None)
    shared = P(("batch", "blk"), None)
    in_specs = (rows, P("batch"), P("batch", None)) + (P(),) * 17 + (rows,)
    out_specs = (
        (rows, rows, P(), P(), shared, P(), P(), shared)
        + (P(),) * 4
        + (shared, P(), shared)
        + (P(),) * 4
    )
    return jax.shard_map(
        functools.partial(shards, mesh.shape["batch"], mesh.shape["blk"]),
        mesh=mesh,
        in_specs=in_specs,
        out_specs=out_specs,
        check_vma=False,
    )
```

time: 1590 us -> 463 us (0.29)
  waiting for transfers between devices: 550 us -> 92 us
  matrix products: 444 us -> 81.2 us
  local copies, waits for them, and re-layouts: 431 us -> 95.6 us
  Pallas kernels: 0 us -> 91 us
  other arithmetic: 92.9 us -> 44.9 us
  starting transfers between devices: 0.93 us -> 46.9 us
  blocking collectives: 42.9 us -> 0 us
    reduce_scatter x5 -> x0, waiting for transfers between devices: 453 us -> none  [the longest x1 142 us: shards(): lax.psum_scatter(d_wfc1, ('batch', 'blk'), scatter_dimension=0, tiled=True)]
    dot_general x30 -> x16, matrix products: 444 us -> 81.2 us  [the longest x8 40.8 us: matmul(): return jnp.dot(left, right, preferred_element_type=F32)]
    reshape x18 -> x10, local copies, waits for them, and re-layouts: 300 us -> 14.5 us  [the longest x2 3.51 us: shards(): inner_high = rel_high[:top_high].T.reshape(heads, SIDE, SIDE)]
    ppermute x0 -> x42, waiting for transfers between devices: none -> 92 us  [the longest x30 92 us: swap(): return lax.ppermute(value, axis, [(i, i ^ bit) for i in range(count)])]
    pallas_call x0 -> x3, Pallas kernels: none -> 91 us  [the longest x1 42.1 us: attention_back(): pl.pallas_call(backward_kernel, grid=(pairs,), out_shape=(flat, flat, fla...]
    psum x1 -> x0, waiting for transfers between devices: 63.5 us -> none  [shards(): lax.psum((d_ln1g, d_ln1b, d_qb, d_vb, d_projb, d_gamma1, d_ln2g, d_ln2b,...]
    convert_element_type x4 -> x0, local copies, waits for them, and re-layouts: 47.8 us -> none  [the longest x2 38.6 us: pair_table(): block = jnp.einsum('hrac,rxy->hxayc', section, offsets, preferred_element...]
    ppermute x0 -> x42, starting transfers between devices: none -> 46.9 us  [the longest x30 28.9 us: swap(): return lax.ppermute(value, axis, [(i, i ^ bit) for i in range(count)])]
  transfers between devices with their start and end apart: 8 -> 42, of which waited for: 6 -> 21; matrix products, arithmetic and copies ran while one was open for 45% -> 27% of each run, Pallas kernels for 0% -> 11%
where the time goes in v1:
time: 463 us; the launch traced here: 455 us
  local copies, waits for them, and re-layouts  95.6 us (21%)
  waiting for transfers between devices  92 us (20%)
  Pallas kernels  91 us (20%)
  matrix products  81.2 us (18%)
  starting transfers between devices  46.9 us (10%)
  other arithmetic  44.9 us (10%)
    ppermute x30, waiting for transfers between devices, swap(): return lax.ppermute(value, axis, [(i, i ^ bit) for i in range(count)])  92 us
    pallas_call x1, Pallas kernels, attention_back(): pl.pallas_call(backward_kernel, grid=(pairs,), out_shape=(flat, flat, fla...  42.1 us
    dot_general x8, matrix products, matmul(): return jnp.dot(left, right, preferred_element_type=F32)  40.8 us
    pallas_call x1, Pallas kernels, attention(): pl.pallas_call(forward_kernel, grid=(pairs,), out_shape=(jax.ShapeDtypeSt...  29.8 us
    ppermute x30, starting transfers between devices, swap(): return lax.ppermute(value, axis, [(i, i ^ bit) for i in range(count)])  28.9 us
    dot_general x4, matrix products, matmul_t(): lax.dot_general(left, right, (((1,), (1,)), ((), ())), preferred_element_...  21.4 us
    unnamed x182, local copies, waits for them, and re-layouts  20 us
    pallas_call x1, Pallas kernels, make_bias(): pl.pallas_call(bias_kernel, grid=(heads,), out_shape=jax.ShapeDtypeStruct...  19.2 us
  transfers between devices with their start and end apart: 42, of which 21 were waited for; matrix products, arithmetic and copies ran while one was open for 27% of the time, Pallas kernels for 11%

profile of v1, /device:TPU:0, one launch (start us, length us, event | category | flops | bytes accessed | tf_op | source)
XLA Modules:
  0.0 454.5 jit_solution(84352082023265995)
XLA Ops:
  3.1 3.0 collective-permute-start
  6.1 2.6 collective-permute-start.1
  54.5 19.2 %bias.1 = bf16[12,640,640]{2,1,0:T(8,128)(2,1)} custom-call(f32[12,3]{1,0:T(8,128)S(1)} %convert_bitcast_fusion.special, bf16[12,48,128]{2,1,0:T(8,128)(2,1)S(1)} %copy-done.13, bf16[128,1152]{1,0:T(8,128)(2,1)S(1)} %copy-done.6, s32[48,1152]{1,0:T(8,128)S(1)} %copy-done.11, f32[640,1]{1,0:T(8,128)S(1)} %copy-done.4, f32[1,640]{1,0:T(1,128)S(1)} %broadcast_in_dim.102.mask), custom_call_target="tpu_custom_call" | custom-call | tf_op jit(solution)/shard_map/bias/pallas_call | solution.py:99
  73.7 2.8 collective-permute-start.8
  81.0 2.6 add_convert_fusion.query.keys.values
  83.7 29.8 %attention.1 = (bf16[12,640,640]{2,1,0:T(8,128)(2,1)}, bf16[640,768]{1,0:T(8,128)(2,1)S(1)}) custom-call(bf16[640,2304]{1,0:T(8,128)(2,1)S(1)} %add_convert_fusion.query.keys.values, bf16[640,2304]{1,0:T(8,128)(2,1)S(1)} %add_convert_fusion.query.keys.values, bf16[640,2304]{1,0:T(8,128)(2,1)S(1)} %add_convert_fusion.query.keys.values, bf16[12,640,640]{2,1,0:T(8,128)(2,1)} %bias.1), custom_call_target="tpu_custom_call" | custom-call | tf_op jit(solution)/shard_map/attention/pallas_call | solution.py:142
  120.6 2.9 convert_reduce_fusion.2
  123.5 21.6 %fusion.2 = (bf16[640,3072]{1,0:T(8,128)(2,1)S(1)}, f32[640,3072]{1,0:T(8,128)}) fusion(f32[3072]{0:T(1024)S(1)} %copy-done.52, bf16[768,3072]{1,0:T(8,128)(2,1)S(1)} %bitcast.266, f32[640,768]{1,0:T(8,128)S(1)} %get-tuple-element.49, f32[768]{0:T(1024)S(1)} %copy-done.62, f32[768]{0:T(1024)S(1)} %copy-done.60, f32[640]{0:T(1024)S(1)} %add_rsqrt_fusion, ...), kind=kOutput, calls=%fused_computation.4 | convolution fusion | flops 3152117760 | bytes 18504704 | tf_op jit(solution)/shard_map/dot_general | solution.py:44
  145.1 9.7 %convert_reduce_fusion = (f32[3072]{0:T(1024)}, bf16[640,3072]{1,0:T(8,128)(2,1)S(1)}) fusion(f32[640,3072]{1,0:T(8,128)} %get-tuple-element.91, f32[3072]{0:T(1024)S(1)} %copy-done.52, bf16[640,768]{1,0:T(8,128)(2,1)S(1)} %get-tuple-element.47, bf16[3072,768]{1,0:T(8,128)(2,1)S(1)} %bitcast.268), kind=kOutput, calls=%fused_computation.11 | convolution fusion | flops 3045454848 | bytes 17522688 | tf_op jit(solution)/shard_map/dot_general | solution.py:48
  154.9 4.2 multiply_reduce_fusion.1
  159.1 6.1 %convert_reduce_fusion.1 = (f32[768]{0:T(1024)}, bf16[640,768]{1,0:T(8,128)(2,1)S(1)}, f32[640,768]{1,0:T(8,128)}, f32[768]{0:T(1024)}, f32[640,768]{1,0:T(8,128)}) fusion(f32[768]{0:T(1024)S(1)} %copy-done.45, f32[640,768]{1,0:T(8,128)S(1)} %get-tuple-element.92, f32[640]{0:T(1024)S(1)} %get-tuple-element.98, f32[640,768]{1,0:T(8,128)S(1)} %get-tuple-element.49, ...), kind=kOutput, calls=%fused_computation.45 | convolution fusion | flops 3027270144 | bytes 19489792 | tf_op jit(solution)/shard_map/dot_general | solution.py:44
  166.7 42.1 %attention_back.1 = (bf16[640,768]{1,0:T(8,128)(2,1)S(1)}, bf16[640,768]{1,0:T(8,128)(2,1)S(1)}, bf16[640,768]{1,0:T(8,128)(2,1)S(1)}, f32[12,48,128]{2,1,0:T(8,128)S(1)}, f32[12,8,640]{2,1,0:T(8,128)S(1)}) custom-call(bf16[640,2304]{1,0:T(8,128)(2,1)} %copy-done.1, bf16[640,2304]{1,0:T(8,128)(2,1)} %copy-done.1, bf16[640,2304]{1,0:T(8,128)(2,1)} %copy-done.1, ...), custom_call_target="tpu_custom_call" | custom-call | tf_op jit(solution)/shard_map/attention_back/pallas_call | solution.py:212
  221.9 6.6 %multiply_reduce_fusion.3 = (f32[768]{0:T(1024)}, f32[640]{0:T(1024)S(1)}, f32[640]{0:T(1024)S(1)}, f32[768]{0:T(1024)}, f32[640,768]{1,0:T(8,128)}) fusion(f32[640,768]{1,0:T(8,128)S(1)} %copy-done.17, f32[640]{0:T(1024)S(1)} %copy-done.65, f32[640]{0:T(1024)S(1)} %broadcast_multiply_fusion.5, f32[768]{0:T(1024)S(1)} %copy-done.54, ...), kind=kOutput, calls=%fused_computation.52 | convolution fusion | flops 2269345024 | bytes 10439680 | tf_op jit(solution)/shard_map/dot_general | solution.py:48
  228.4 4.7 %convolution_convert_fusion.2 = bf16[768,2304]{1,0:T(8,128)(2,1)} fusion(bf16[640,2304]{1,0:T(8,128)(2,1)S(1)} %copy-done.36, f32[640,768]{1,0:T(8,128)S(1)} %copy-done.17, f32[768]{0:T(1024)S(1)} %copy-done.59, f32[768]{0:T(1024)S(1)} %copy-done.54, f32[640]{0:T(1024)S(1)} %copy-done.65, f32[640]{0:T(1024)S(1)} %broadcast_multiply_fusion.5), kind=kOutput, calls=%fused_computation.30 | convolution fusion | flops 2269151232 | bytes 8465408 | tf_op jit(solution)/shard_map/dot_general | solution.py:52
  236.4 6.4 %convolution_convert_fusion.1 = bf16[768,3072]{1,0:T(8,128)(2,1)} fusion(bf16[640,3072]{1,0:T(8,128)(2,1)S(1)} %copy-done.79, f32[640,768]{1,0:T(8,128)S(1)} %copy-done.20, f32[768]{0:T(1024)S(1)} %copy-done.63, f32[768]{0:T(1024)S(1)} %copy-done.61, f32[640]{0:T(1024)S(1)} %copy-done.69, f32[640]{0:T(1024)S(1)} %copy-done.47), kind=kOutput, calls=%fused_computation.29 | convolution fusion | flops 3024715776 | bytes 10628096 | tf_op jit(solution)/shard_map/dot_general | solution.py:52
  242.8 5.7 %convolution_convert_fusion = bf16[3072,768]{1,0:T(8,128)(2,1)} fusion(bf16[640,3072]{1,0:T(8,128)(2,1)S(1)} %copy-done.77, bf16[640,768]{1,0:T(8,128)(2,1)S(1)} %copy-done.35), kind=kOutput, calls=%fused_computation.28 | convolution fusion | flops 3022258176 | bytes 9633792 | tf_op jit(solution)/shard_map/dot_general | solution.py:52
  253.6 2.9 collective-permute-start.5
  288.4 3.2 fusion.27
  291.6 4.4 constant_dynamic-slice_fusion.3
  312.5 8.6 %collective-permute-done.31 = f32[64,128]{1,0:T(8,128)S(1)} collective-permute-done((f32[64,128]{1,0:T(8,128)S(1)}, f32[64,128]{1,0:T(8,128)S(1)}, u32[]{:S(2)}, u32[]{:S(2)}) %collective-permute-start.31) | collective-permute-done | bytes 32800 | tf_op jit(solution)/shard_map/ppermute | solution.py:263
  327.8 4.4 collective-permute-done.13
  335.5 3.4 collective-permute-done.14
  348.0 2.9 collective-permute-start.16
  365.8 9.7 %collective-permute-done.18 = bf16[2,2,2,24,2304]{4,3,1,2,0:T(8,128)(2,1)} collective-permute-done((bf16[2,2,2,24,2304]{4,3,1,2,0:T(8,128)(2,1)}, bf16[2,2,2,24,2304]{4,3,1,2,0:T(8,128)(2,1)}, u32[]{:S(2)}, u32[]{:S(2)}) %collective-permute-start.18) | collective-permute-done | bytes 884768 | tf_op jit(solution)/shard_map/ppermute | solution.py:263
  378.6 2.6 fusion.17
  382.5 5.9 %collective-permute-done.19 = bf16[2,2,24,2304]{3,2,0,1:T(8,128)(2,1)S(1)} collective-permute-done((bf16[2,2,24,2304]{3,2,0,1:T(8,128)(2,1)S(1)}, bf16[2,2,24,2304]{3,2,0,1:T(8,128)(2,1)S(1)}, u32[]{:S(2)}, u32[]{:S(2)}) %collective-permute-start.19) | collective-permute-done | bytes 442400 | tf_op jit(solution)/shard_map/ppermute | solution.py:263
  395.3 12.7 %collective-permute-done.33 = bf16[2,2,2,24,3072]{4,3,1,2,0:T(8,128)(2,1)S(1)} collective-permute-done((bf16[2,2,2,24,3072]{4,3,1,2,0:T(8,128)(2,1)S(1)}, bf16[2,2,2,24,3072]{4,3,1,2,0:T(8,128)(2,1)S(1)}, u32[]{:S(2)}, u32[]{:S(2)}) %collective-permute-start.33) | collective-permute-done | bytes 1179680 | tf_op jit(solution)/shard_map/ppermute | solution.py:263
  409.9 10.1 %collective-permute-done.38 = bf16[2,2,2,96,768]{4,3,1,2,0:T(8,128)(2,1)S(1)} collective-permute-done((bf16[2,2,2,96,768]{4,3,1,2,0:T(8,128)(2,1)S(1)}, bf16[2,2,2,96,768]{4,3,1,2,0:T(8,128)(2,1)S(1)}, u32[]{:S(2)}, u32[]{:S(2)}) %collective-permute-start.38) | collective-permute-done | bytes 1179680 | tf_op jit(solution)/shard_map/ppermute | solution.py:263
  421.8 8.0 %collective-permute-done.34 = bf16[2,2,24,3072]{3,2,0,1:T(8,128)(2,1)S(1)} collective-permute-done((bf16[2,2,24,3072]{3,2,0,1:T(8,128)(2,1)S(1)}, bf16[2,2,24,3072]{3,2,0,1:T(8,128)(2,1)S(1)}, u32[]{:S(2)}, u32[]{:S(2)}) %collective-permute-start.34) | collective-permute-done | bytes 589856 | tf_op jit(solution)/shard_map/ppermute | solution.py:263
  432.6 8.3 %collective-permute-done.35 = bf16[2,24,3072]{2,1,0:T(8,128)(2,1)S(1)} collective-permute-done((bf16[2,24,3072]{2,1,0:T(8,128)(2,1)S(1)}, bf16[2,24,3072]{2,1,0:T(8,128)(2,1)S(1)}, u32[]{:S(2)}, u32[]{:S(2)}) %collective-permute-start.35) | collective-permute-done | bytes 294944 | tf_op jit(solution)/shard_map/ppermute | solution.py:263
  441.3 3.3 collective-permute-done.40
  446.7 3.5 collective-permute-done.36
  (400 shorter events, 187.6 us)
Async XLA Ops:
  3.1 70.6 %collective-permute-start = (bf16[160,768]{1,0:T(8,128)(2,1)}, bf16[160,768]{1,0:T(8,128)(2,1)}, u32[]{:S(2)}, u32[]{:S(2)}) collective-permute-start(bf16[160,768]{1,0:T(8,128)(2,1)} %get-tuple-element.72), channel_id=1, source_target_pairs={{0,1},{1,2},{2,3},{3,0},{4,5},{5,6},{6,7},{7,4},{8,9},{9,10},{10,1... | collective-permute-start | bytes 737288 | tf_op jit(solution)/shard_map/ppermute | solution.py:253
  6.1 71.4 %collective-permute-start.1 = (bf16[160,768]{1,0:T(8,128)(2,1)}, bf16[160,768]{1,0:T(8,128)(2,1)}, u32[]{:S(2)}, u32[]{:S(2)}) collective-permute-start(bf16[160,768]{1,0:T(8,128)(2,1)} %get-tuple-element.74), channel_id=1, source_target_pairs={{0,2},{1,3},{2,0},{3,1},{4,6},{5,7},{6,4},{7,5},{8,10},{9,11},{10,... | collective-permute-start | bytes 737288 | tf_op jit(solution)/shard_map/ppermute | solution.py:253
  8.7 69.8 %collective-permute-start.2 = (bf16[160,768]{1,0:T(8,128)(2,1)}, bf16[160,768]{1,0:T(8,128)(2,1)}, u32[]{:S(2)}, u32[]{:S(2)}) collective-permute-start(bf16[160,768]{1,0:T(8,128)(2,1)} %get-tuple-element.71), channel_id=1, source_target_pairs={{0,3},{1,0},{2,1},{3,2},{4,7},{5,4},{6,5},{7,6},{8,11},{9,8},{10,9... | collective-permute-start | bytes 737288 | tf_op jit(solution)/shard_map/ppermute | solution.py:253
  12.0 103.8 %collective-permute-start.6 = (bf16[160,768]{1,0:T(8,128)(2,1)}, bf16[160,768]{1,0:T(8,128)(2,1)}, u32[]{:S(2)}, u32[]{:S(2)}) collective-permute-start(bf16[160,768]{1,0:T(8,128)(2,1)} %get-tuple-element.64), channel_id=1, source_target_pairs={{0,1},{1,2},{2,3},{3,0},{4,5},{5,6},{6,7},{7,4},{8,9},{9,10},{10,1... | collective-permute-start | bytes 737288 | tf_op jit(solution)/shard_map/ppermute | solution.py:253
  12.7 105.5 %collective-permute-start.7 = (bf16[160,768]{1,0:T(8,128)(2,1)}, bf16[160,768]{1,0:T(8,128)(2,1)}, u32[]{:S(2)}, u32[]{:S(2)}) collective-permute-start(bf16[160,768]{1,0:T(8,128)(2,1)} %get-tuple-element.66), channel_id=1, source_target_pairs={{0,2},{1,3},{2,0},{3,1},{4,6},{5,7},{6,4},{7,5},{8,10},{9,11},{10,... | collective-permute-start | bytes 737288 | tf_op jit(solution)/shard_map/ppermute | solution.py:253
  73.7 46.1 %collective-permute-start.8 = (bf16[160,768]{1,0:T(8,128)(2,1)S(1)}, bf16[160,768]{1,0:T(8,128)(2,1)S(1)}, u32[]{:S(2)}, u32[]{:S(2)}) collective-permute-start(bf16[160,768]{1,0:T(8,128)(2,1)S(1)} %copy-done.39), channel_id=1, source_target_pairs={{0,3},{1,0},{2,1},{3,2},{4,7},{5,4},{6,5},{7,6},{8,11},{9,8},{10,9... | collective-permute-start | bytes 737288 | tf_op jit(solution)/shard_map/ppermute | solution.py:253
  251.7 70.7 %collective-permute-start.3 = (bf16[160,768]{1,0:T(8,128)(2,1)}, bf16[160,768]{1,0:T(8,128)(2,1)}, u32[]{:S(2)}, u32[]{:S(2)}) collective-permute-start(bf16[160,768]{1,0:T(8,128)(2,1)} %get-tuple-element.69), channel_id=1, source_target_pairs={{0,1},{1,2},{2,3},{3,0},{4,5},{5,6},{6,7},{7,4},{8,9},{9,10},{10,1... | collective-permute-start | bytes 737288 | tf_op jit(solution)/shard_map/ppermute | solution.py:253
  252.2 71.2 %collective-permute-start.4 = (bf16[160,768]{1,0:T(8,128)(2,1)}, bf16[160,768]{1,0:T(8,128)(2,1)}, u32[]{:S(2)}, u32[]{:S(2)}) collective-permute-start(bf16[160,768]{1,0:T(8,128)(2,1)} %get-tuple-element.68), channel_id=1, source_target_pairs={{0,2},{1,3},{2,0},{3,1},{4,6},{5,7},{6,4},{7,5},{8,10},{9,11},{10,... | collective-permute-start | bytes 737288 | tf_op jit(solution)/shard_map/ppermute | solution.py:253
  253.6 71.0 %collective-permute-start.5 = (bf16[160,768]{1,0:T(8,128)(2,1)}, bf16[160,768]{1,0:T(8,128)(2,1)}, u32[]{:S(2)}, u32[]{:S(2)}) collective-permute-start(bf16[160,768]{1,0:T(8,128)(2,1)} %get-tuple-element.67), channel_id=1, source_target_pairs={{0,3},{1,0},{2,1},{3,2},{4,7},{5,4},{6,5},{7,6},{8,11},{9,8},{10,9... | collective-permute-start | bytes 737288 | tf_op jit(solution)/shard_map/ppermute | solution.py:253
  278.7 32.7 %collective-permute-start.12 = (f32[304,128]{1,0:T(8,128)S(1)}, f32[304,128]{1,0:T(8,128)S(1)}, u32[]{:S(2)}, u32[]{:S(2)}) collective-permute-start(f32[304,128]{1,0:T(8,128)S(1)} %pad_bitcast_fusion), channel_id=1, source_target_pairs={{0,4},{4,0},{8,12},{12,8},{16,20},{20,16},{24,28},{28,24},{1,5},{5... | collective-permute-start | bytes 466952 | tf_op jit(solution)/shard_map/ppermute | solution.py:263
  287.9 8.4 %collective-permute-start.27 = (f32[64,128]{1,0:T(8,128)S(1)}, f32[64,128]{1,0:T(8,128)S(1)}, u32[]{:S(2)}, u32[]{:S(2)}) collective-permute-start(f32[64,128]{1,0:T(8,128)S(1)} %pad_bitcast_fusion.1), channel_id=1, source_target_pairs={{0,4},{4,0},{8,12},{12,8},{16,20},{20,16},{24,28},{28,24},{1,5},{5... | collective-permute-start | bytes 98312 | tf_op jit(solution)/shard_map/ppermute | solution.py:263
  309.4 24.2 %collective-permute-start.9 = (bf16[160,768]{1,0:T(8,128)(2,1)S(1)}, bf16[160,768]{1,0:T(8,128)(2,1)S(1)}, u32[]{:S(2)}, u32[]{:S(2)}) collective-permute-start(bf16[160,768]{1,0:T(8,128)(2,1)S(1)} %get-tuple-element.61), channel_id=1, source_target_pairs={{0,1},{1,2},{2,3},{3,0},{4,5},{5,6},{6,7},{7,4},{8,9},{9,10},{10,1... | collective-permute-start | bytes 737288 | tf_op jit(solution)/shard_map/ppermute | solution.py:253
  311.4 9.7 %collective-permute-start.31 = (f32[64,128]{1,0:T(8,128)S(1)}, f32[64,128]{1,0:T(8,128)S(1)}, u32[]{:S(2)}, u32[]{:S(2)}) collective-permute-start(f32[64,128]{1,0:T(8,128)S(1)} %add.419), channel_id=1, source_target_pairs={{0,2},{1,3},{2,0},{3,1},{4,6},{5,7},{6,4},{7,5},{8,10},{9,11},{10,... | collective-permute-start | bytes 98312 | tf_op jit(solution)/shard_map/ppermute | solution.py:263
  321.1 21.6 %collective-permute-start.10 = (bf16[160,768]{1,0:T(8,128)(2,1)S(1)}, bf16[160,768]{1,0:T(8,128)(2,1)S(1)}, u32[]{:S(2)}, u32[]{:S(2)}) collective-permute-start(bf16[160,768]{1,0:T(8,128)(2,1)S(1)} %get-tuple-element.60), channel_id=1, source_target_pairs={{0,2},{1,3},{2,0},{3,1},{4,6},{5,7},{6,4},{7,5},{8,10},{9,11},{10,... | collective-permute-start | bytes 737288 | tf_op jit(solution)/shard_map/ppermute | solution.py:253
  323.4 30.3 %collective-permute-start.11 = (bf16[160,768]{1,0:T(8,128)(2,1)S(1)}, bf16[160,768]{1,0:T(8,128)(2,1)S(1)}, u32[]{:S(2)}, u32[]{:S(2)}) collective-permute-start(bf16[160,768]{1,0:T(8,128)(2,1)S(1)} %get-tuple-element.59), channel_id=1, source_target_pairs={{0,3},{1,0},{2,1},{3,2},{4,7},{5,4},{6,5},{7,6},{8,11},{9,8},{10,9... | collective-permute-start | bytes 737288 | tf_op jit(solution)/shard_map/ppermute | solution.py:253
  324.7 26.3 %collective-permute-start.17 = (bf16[2,2,2,2,24,2304]{5,4,2,3,1,0:T(8,128)(2,1)S(1)}, bf16[2,2,2,2,24,2304]{5,4,2,3,1,0:T(8,128)(2,1)S(1)}, u32[]{:S(2)}, u32[]{:S(2)}) collective-permute-start(bf16[2,2,2,2,24,2304]{5,4,2,3,1,0:T(8,128)(2,1)S(1)} %bitcast.249), channel_id=1, source_target_pairs={{0,4},{4,0},{8,12},{12,8},{16,20},{20,16},{24,28},{28,24},{1,5},{5... | collective-permute-start | bytes 5308424 | tf_op jit(solution)/shard_map/ppermute | solution.py:263
  332.2 8.1 %collective-permute-start.23 = (bf16[2,2,2,24,768]{4,3,1,2,0:T(8,128)(2,1)S(1)}, bf16[2,2,2,24,768]{4,3,1,2,0:T(8,128)(2,1)S(1)}, u32[]{:S(2)}, u32[]{:S(2)}) collective-permute-start(bf16[2,2,2,24,768]{4,3,1,2,0:T(8,128)(2,1)S(1)} %dynamic-slice_bitcast_fusion.8), channel_id=1, source_target_pairs={{0,8},{4,12},{8,0},{12,4},{16,24},{20,28},{24,16},{28,20},{1,9},{5... | collective-permute-start | bytes 884744 | tf_op jit(solution)/shard_map/ppermute | solution.py:263
  338.9 39.7 %collective-permute-start.32 = (bf16[2,2,2,2,24,3072]{5,4,2,3,1,0:T(8,128)(2,1)}, bf16[2,2,2,2,24,3072]{5,4,2,3,1,0:T(8,128)(2,1)}, u32[]{:S(2)}, u32[]{:S(2)}) collective-permute-start(bf16[2,2,2,2,24,3072]{5,4,2,3,1,0:T(8,128)(2,1)} %bitcast.239), channel_id=1, source_target_pairs={{0,4},{4,0},{8,12},{12,8},{16,20},{20,16},{24,28},{28,24},{1,5},{5... | collective-permute-start | bytes 7077896 | tf_op jit(solution)/shard_map/ppermute | solution.py:263
  345.8 42.8 %collective-permute-start.37 = (bf16[2,2,2,2,96,768]{5,4,2,3,0,1:T(8,128)(2,1)}, bf16[2,2,2,2,96,768]{5,4,2,3,0,1:T(8,128)(2,1)}, u32[]{:S(2)}, u32[]{:S(2)}) collective-permute-start(bf16[2,2,2,2,96,768]{5,4,2,3,0,1:T(8,128)(2,1)} %bitcast.238), channel_id=1, source_target_pairs={{0,4},{4,0},{8,12},{12,8},{16,20},{20,16},{24,28},{28,24},{1,5},{5... | collective-permute-start | bytes 7077896 | tf_op jit(solution)/shard_map/ppermute | solution.py:263
  348.0 9.0 %collective-permute-start.16 = (f32[304,128]{1,0:T(8,128)S(1)}, f32[304,128]{1,0:T(8,128)S(1)}, u32[]{:S(2)}, u32[]{:S(2)}) collective-permute-start(f32[304,128]{1,0:T(8,128)S(1)} %add.394), channel_id=1, source_target_pairs={{0,2},{1,3},{2,0},{3,1},{4,6},{5,7},{6,4},{7,5},{8,10},{9,11},{10,... | collective-permute-start | bytes 466952 | tf_op jit(solution)/shard_map/ppermute | solution.py:263
  350.9 6.2 %collective-permute-start.25 = (bf16[2,24,768]{2,1,0:T(8,128)(2,1)S(1)}, bf16[2,24,768]{2,1,0:T(8,128)(2,1)S(1)}, u32[]{:S(2)}, u32[]{:S(2)}) collective-permute-start(bf16[2,24,768]{2,1,0:T(8,128)(2,1)S(1)} %dynamic-slice_bitcast_fusion.26), channel_id=1, source_target_pairs={{0,1},{1,0},{2,3},{3,2},{4,5},{5,4},{6,7},{7,6},{8,9},{9,8},{10,11... | collective-permute-start | bytes 221192 | tf_op jit(solution)/shard_map/ppermute | solution.py:263
  353.7 21.8 %collective-permute-start.18 = (bf16[2,2,2,24,2304]{4,3,1,2,0:T(8,128)(2,1)}, bf16[2,2,2,24,2304]{4,3,1,2,0:T(8,128)(2,1)}, u32[]{:S(2)}, u32[]{:S(2)}) collective-permute-start(bf16[2,2,2,24,2304]{4,3,1,2,0:T(8,128)(2,1)} %dynamic-slice_bitcast_fusion.2), channel_id=1, source_target_pairs={{0,16},{4,20},{8,24},{12,28},{16,0},{20,4},{24,8},{28,12},{1,17},{... | collective-permute-start | bytes 2654216 | tf_op jit(solution)/shard_map/ppermute | solution.py:263
  377.2 11.2 %collective-permute-start.19 = (bf16[2,2,24,2304]{3,2,0,1:T(8,128)(2,1)S(1)}, bf16[2,2,24,2304]{3,2,0,1:T(8,128)(2,1)S(1)}, u32[]{:S(2)}, u32[]{:S(2)}) collective-permute-start(bf16[2,2,24,2304]{3,2,0,1:T(8,128)(2,1)S(1)} %dynamic-slice_bitcast_fusion.5), channel_id=1, source_target_pairs={{0,8},{4,12},{8,0},{12,4},{16,24},{20,28},{24,16},{28,20},{1,9},{5... | collective-permute-start | bytes 1327112 | tf_op jit(solution)/shard_map/ppermute | solution.py:263
  381.3 26.7 %collective-permute-start.33 = (bf16[2,2,2,24,3072]{4,3,1,2,0:T(8,128)(2,1)S(1)}, bf16[2,2,2,24,3072]{4,3,1,2,0:T(8,128)(2,1)S(1)}, u32[]{:S(2)}, u32[]{:S(2)}) collective-permute-start(bf16[2,2,2,24,3072]{4,3,1,2,0:T(8,128)(2,1)S(1)} %dynamic-slice_bitcast_fusion.1), channel_id=1, source_target_pairs={{0,16},{4,20},{8,24},{12,28},{16,0},{20,4},{24,8},{28,12},{1,17},{... | collective-permute-start | bytes 3538952 | tf_op jit(solution)/shard_map/ppermute | solution.py:263
  391.1 29.0 %collective-permute-start.38 = (bf16[2,2,2,96,768]{4,3,1,2,0:T(8,128)(2,1)S(1)}, bf16[2,2,2,96,768]{4,3,1,2,0:T(8,128)(2,1)S(1)}, u32[]{:S(2)}, u32[]{:S(2)}) collective-permute-start(bf16[2,2,2,96,768]{4,3,1,2,0:T(8,128)(2,1)S(1)} %dynamic-slice_bitcast_fusion), channel_id=1, source_target_pairs={{0,8},{4,12},{8,0},{12,4},{16,24},{20,28},{24,16},{28,20},{1,9},{5... | collective-permute-start | bytes 3538952 | tf_op jit(solution)/shard_map/ppermute | solution.py:263
  394.6 14.6 %collective-permute-start.21 = (bf16[24,2304]{1,0:T(8,128)(2,1)S(1)}, bf16[24,2304]{1,0:T(8,128)(2,1)S(1)}, u32[]{:S(2)}, u32[]{:S(2)}) collective-permute-start(bf16[24,2304]{1,0:T(8,128)(2,1)S(1)} %dynamic-slice_bitcast_fusion.25), channel_id=1, source_target_pairs={{0,2},{1,3},{2,0},{3,1},{4,6},{5,7},{6,4},{7,5},{8,10},{9,11},{10,... | collective-permute-start | bytes 331784 | tf_op jit(solution)/shard_map/ppermute | solution.py:263
  408.5 21.3 %collective-permute-start.34 = (bf16[2,2,24,3072]{3,2,0,1:T(8,128)(2,1)S(1)}, bf16[2,2,24,3072]{3,2,0,1:T(8,128)(2,1)S(1)}, u32[]{:S(2)}, u32[]{:S(2)}) collective-permute-start(bf16[2,2,24,3072]{3,2,0,1:T(8,128)(2,1)S(1)} %dynamic-slice_bitcast_fusion.4), channel_id=1, source_target_pairs={{0,8},{4,12},{8,0},{12,4},{16,24},{20,28},{24,16},{28,20},{1,9},{5... | collective-permute-start | bytes 1769480 | tf_op jit(solution)/shard_map/ppermute | solution.py:263
  420.4 11.4 %collective-permute-start.39 = (bf16[2,2,96,768]{3,2,0,1:T(8,128)(2,1)S(1)}, bf16[2,2,96,768]{3,2,0,1:T(8,128)(2,1)S(1)}, u32[]{:S(2)}, u32[]{:S(2)}) collective-permute-start(bf16[2,2,96,768]{3,2,0,1:T(8,128)(2,1)S(1)} %dynamic-slice_bitcast_fusion.3), channel_id=1, source_target_pairs={{0,16},{4,20},{8,24},{12,28},{16,0},{20,4},{24,8},{28,12},{1,17},{... | collective-permute-start | bytes 1769480 | tf_op jit(solution)/shard_map/ppermute | solution.py:263
  430.0 10.9 %collective-permute-start.35 = (bf16[2,24,3072]{2,1,0:T(8,128)(2,1)S(1)}, bf16[2,24,3072]{2,1,0:T(8,128)(2,1)S(1)}, u32[]{:S(2)}, u32[]{:S(2)}) collective-permute-start(bf16[2,24,3072]{2,1,0:T(8,128)(2,1)S(1)} %dynamic-slice_bitcast_fusion.7), channel_id=1, source_target_pairs={{0,1},{1,0},{2,3},{3,2},{4,5},{5,4},{6,7},{7,6},{8,9},{9,8},{10,11... | collective-permute-start | bytes 884744 | tf_op jit(solution)/shard_map/ppermute | solution.py:263
  432.0 12.7 %collective-permute-start.40 = (bf16[2,96,768]{2,1,0:T(8,128)(2,1)S(1)}, bf16[2,96,768]{2,1,0:T(8,128)(2,1)S(1)}, u32[]{:S(2)}, u32[]{:S(2)}) collective-permute-start(bf16[2,96,768]{2,1,0:T(8,128)(2,1)S(1)} %dynamic-slice_bitcast_fusion.6), channel_id=1, source_target_pairs={{0,1},{1,0},{2,3},{3,2},{4,5},{5,4},{6,7},{7,6},{8,9},{9,8},{10,11... | collective-permute-start | bytes 884744 | tf_op jit(solution)/shard_map/ppermute | solution.py:263
  441.0 9.2 %collective-permute-start.36 = (bf16[24,3072]{1,0:T(8,128)(2,1)S(1)}, bf16[24,3072]{1,0:T(8,128)(2,1)S(1)}, u32[]{:S(2)}, u32[]{:S(2)}) collective-permute-start(bf16[24,3072]{1,0:T(8,128)(2,1)S(1)} %dynamic-slice_bitcast_fusion.23), channel_id=1, source_target_pairs={{0,2},{1,3},{2,0},{3,1},{4,6},{5,7},{6,4},{7,5},{8,10},{9,11},{10,... | collective-permute-start | bytes 442376 | tf_op jit(solution)/shard_map/ppermute | solution.py:263
  444.7 8.6 %collective-permute-start.41 = (bf16[96,768]{1,0:T(8,128)(2,1)S(1)}, bf16[96,768]{1,0:T(8,128)(2,1)S(1)}, u32[]{:S(2)}, u32[]{:S(2)}) collective-permute-start(bf16[96,768]{1,0:T(8,128)(2,1)S(1)} %dynamic-slice_bitcast_fusion.22), channel_id=1, source_target_pairs={{0,2},{1,3},{2,0},{3,1},{4,6},{5,7},{6,4},{7,5},{8,10},{9,11},{10,... | collective-permute-start | bytes 442376 | tf_op jit(solution)/shard_map/ppermute | solution.py:263
  (96 other events, 1188.2 us)
